TPU v7x, 128 devices: a whole 4x4x4 slice. The times are simulated.
128 devices in a mesh: chan: 64 (over x, y, z_lo, core), quad: 2 (over z_hi).
Axes of the slice: x: 4, y: 4, z: 4 (z_hi: 2, z_lo: 2; z = z_hi * 2 + z_lo), core: 2. Of those that a mesh axis runs over, the one named last changes fastest.
Arguments:
- voltages: float32 [2, 512, 2, 2, 8416], P('quad', 'chan'), may hold values from -6 to 6
- filter_taps: float32 [8, 32], replicated, may hold values from -0.375 to 0.375
- phases: int32 [64, 512, 1024], P('chan', None, 'quad'), may hold values from 0 to 255
Outputs:
- visibilities: float32 [64, 2, 1024, 1024], P('chan', None, 'quad')
- beam_power: float32 [64, 512, 256], P('chan', 'quad')
All inputs are finite; a program needn't handle non-finite values.
Results may differ from a plain program's by a relative error of at most 0.0001.
Values sent between devices are 32-bit elements; how exact they have to be, the bound alone decides.
A program may use at most 128 MiB of HBM per device.

v0:
```python
import math

import jax
import jax.numpy as jnp
from jax import lax
from jax.sharding import PartitionSpec as P

DISHES = 1024
FINE = 32
TAPS = 8
PHASE_LEVELS = 256
MB = 2
SB = 128


highest = lax.Precision.HIGHEST


def dft_matrix():
    index_n = jnp.arange(FINE, dtype=jnp.int32)
    product = index_n[:, None] * index_n[None, :] % FINE
    angles = product.astype(jnp.float32) * (2.0 * math.pi / FINE)
    cosine = jnp.cos(angles)
    sine = jnp.sin(angles)
    return jnp.stack([jnp.stack([cosine, sine]), jnp.stack([-sine, cosine])])


def filter_bank(voltages, filter_taps, first_spec, length):
    dish_count = voltages.shape[1]
    coarse_count = voltages.shape[2]
    window = voltages[0, :, :, :, first_spec * FINE : (first_spec + length + TAPS - 1) * FINE]
    frames = window.reshape(dish_count, coarse_count, 2, length + TAPS - 1, FINE)
    filtered = jnp.zeros((dish_count, coarse_count, 2, length, FINE), jnp.float32)
    for tap_index in range(TAPS):
        filtered = (
            filtered + filter_taps[tap_index] * frames[:, :, :, tap_index : tap_index + length, :]
        )
    spectra = jnp.einsum("dbisn,jink->bkdjs", filtered, dft_matrix(), precision=highest)
    return spectra.reshape(coarse_count * FINE, dish_count, 2, length)


def steering_gains(phase_block):
    steer_angle = phase_block.astype(jnp.float32) * (2.0 * math.pi / PHASE_LEVELS)
    cosine = jnp.cos(steer_angle)
    sine = jnp.sin(steer_angle)
    return jnp.stack([jnp.stack([cosine, sine], -1), jnp.stack([-sine, cosine], -1)], axis=1)


def make_visit(own_rows, column_block):
    left_side = own_rows.reshape(own_rows.shape[0], own_rows.shape[1], -1)
    flat = column_block.reshape(column_block.shape[0], column_block.shape[1], -1)
    swapped = jnp.concatenate([-column_block[:, :, 1], column_block[:, :, 0]], axis=-1)
    right_side = jnp.stack([flat, swapped], axis=1)
    return jnp.einsum("crk,cvqk->cvrq", left_side, right_side, precision=highest)


def per_device(voltages, filter_taps, phases):
    own_blocks = []
    for batch in range(MB):
        local_part = filter_bank(voltages, filter_taps, batch * SB, SB)
        own_blocks.append(
            lax.all_to_all(local_part, "chan", split_axis=0, concat_axis=1, tiled=True)
        )
    for batch in range(MB):
        own_rows = own_blocks[batch]
        batch_terms = make_visit(own_rows, lax.all_gather(own_rows, "quad", axis=1, tiled=True))
        visible = batch_terms if batch == 0 else visible + batch_terms
    visibilities = visible / (MB * SB)
    own_all = jnp.concatenate(own_blocks, axis=3)
    gains = steering_gains(phases)
    partial_beams = jnp.einsum("cvbri,cris->cvbs", gains, own_all, precision=highest)
    shares = lax.psum_scatter(partial_beams, "quad", scatter_dimension=2, tiled=True)
    beam_power = (shares[:, 0] * shares[:, 0] + shares[:, 1] * shares[:, 1]) / DISHES
    return (visibilities, beam_power)


def solution(mesh):
    placed = (P("quad", "chan", None, None, None), P(), P("chan", None, "quad"))
    return jax.shard_map(
        per_device,
        mesh=mesh,
        in_specs=placed,
        out_specs=(P("chan", None, "quad", None), P("chan", "quad", None)),
        check_vma=False,
    )
```

profile of v0, /device:TPU:1, one launch (start us, length us, event | category | flops | bytes accessed | tf_op | source)
XLA Modules:
  0.0 167.8 jit_solution(9185713223130764932)
XLA Ops:
  11.6 6.0 %fusion.84 = (f32[8,2,2,128,32]{4,3,2,1,0:T(8,128)}, f32[8,2,2,128,32]{4,3,2,1,0:T(8,128)}, f32[8,2,2,128,32]{4,3,2,1,0:T(8,128)}, f32[8,2,2,128,32]{4,3,2,1,0:T...) fusion(f32[8,2,2,135,32]{4,3,2,1,0:T(8,128)S(1)} %reshape.213), kind=kLoop, calls=%fused_computation.118 | loop fusion | bytes 8388608 | tf_op jit(solution)/shard_map/slice | solution.py:36
  21.3 3.1 %copy.102 = f32[8,2,2,128,32]{3,4,2,1,0:T(8,128)} copy(f32[8,2,2,128,32]{4,3,2,1,0:T(8,128)} %get-tuple-element.17) | data formatting | bytes 1048576
  24.4 3.0 %copy.95 = f32[8,2,2,128,32]{3,4,2,1,0:T(8,128)} copy(f32[8,2,2,128,32]{4,3,2,1,0:T(8,128)} %get-tuple-element.10) | data formatting | bytes 1048576
  28.8 3.1 %copy.97 = f32[8,2,2,128,32]{3,4,2,1,0:T(8,128)} copy(f32[8,2,2,128,32]{4,3,2,1,0:T(8,128)} %get-tuple-element.15) | data formatting | bytes 1048576
  31.9 3.0 %copy.98 = f32[8,2,2,128,32]{3,4,2,1,0:T(8,128)} copy(f32[8,2,2,128,32]{4,3,2,1,0:T(8,128)} %get-tuple-element.14) | data formatting | bytes 1048576
  36.3 2.9 %fusion.17 = f32[2,32,8,2,128,1]{4,1,5,3,2,0:T(8,128)S(1)} fusion(f32[8,2,2,128,32]{3,4,2,1,0:T(8,128)} %copy.102, f32[8,2,2,128,32]{3,4,2,1,0:T(8,128)} %copy.101, f32[8,2,2,128,32]{3,4,2,1,0:T(8,128)S(1)} %copy.100, f32[8,2,2,128,32]{3,4,2,1,0:T(8,128)} %copy.99, f32[8,2,2,128,32]{3,4,2,1,0:T(8,128)} %copy.98, f32[8,2,2,128,32]{3,4,2,1,0:T(8,128)} %copy.97, ...), kind=kOutput, calls=%fused_computation.33 | convolution fusion | flops 102633472 | bytes 4736000 | tf_op jit(solution)/shard_map/dbisn,jink->bkdjs/dot_general | solution.py:38
  40.4 10.3 %all-to-all-start.1 = ((f32[64,8,2,128]{3,1,2,0:T(8,128)}), f32[64,8,2,128]{3,1,2,0:T(8,128)S(1)}, u32[]{:S(2)}, u32[]{:S(2)}) async-start(f32[64,8,2,128]{3,1,2,0:T(8,128)} %copy.74), calls=%async_computation.1 | async-start | bytes 1048576 | tf_op jit(solution)/shard_map/all_to_all | solution.py:62
  51.8 11.4 %all-to-all-done.1 = f32[64,8,2,128]{3,1,2,0:T(8,128)S(1)} async-done(((f32[64,8,2,128]{3,1,2,0:T(8,128)}), f32[64,8,2,128]{3,1,2,0:T(8,128)S(1)}, u32[]{:S(2)}, u32[]{:S(2)}) %all-to-all-start.1) | async-done | bytes 524320 | tf_op jit(solution)/shard_map/all_to_all | solution.py:62
  64.3 6.0 %fusion.85 = (f32[8,2,2,128,32]{4,3,2,1,0:T(8,128)}, f32[8,2,2,128,32]{4,3,2,1,0:T(8,128)}, f32[8,2,2,128,32]{4,3,2,1,0:T(8,128)}, f32[8,2,2,128,32]{4,3,2,1,0:T...) fusion(f32[8,2,2,135,32]{4,3,2,1,0:T(8,128)S(1)} %reshape.212), kind=kLoop, calls=%fused_computation.119 | loop fusion | bytes 8388608 | tf_op jit(solution)/shard_map/slice | solution.py:36
  74.1 3.2 %copy.89 = f32[8,2,2,128,32]{3,4,2,1,0:T(8,128)} copy(f32[8,2,2,128,32]{4,3,2,1,0:T(8,128)} %get-tuple-element.23) | data formatting | bytes 1048576
  77.2 3.0 %copy.90 = f32[8,2,2,128,32]{3,4,2,1,0:T(8,128)} copy(f32[8,2,2,128,32]{4,3,2,1,0:T(8,128)} %get-tuple-element.22) | data formatting | bytes 1048576
  81.6 3.1 %copy.92 = f32[8,2,2,128,32]{3,4,2,1,0:T(8,128)} copy(f32[8,2,2,128,32]{4,3,2,1,0:T(8,128)} %get-tuple-element.20) | data formatting | bytes 1048576
  84.8 3.0 %copy.93 = f32[8,2,2,128,32]{3,4,2,1,0:T(8,128)} copy(f32[8,2,2,128,32]{4,3,2,1,0:T(8,128)} %get-tuple-element.19) | data formatting | bytes 1048576
  89.1 2.9 %fusion.19 = f32[2,32,8,2,128,1]{4,1,5,3,2,0:T(8,128)S(1)} fusion(f32[8,2,2,128,32]{3,4,2,1,0:T(8,128)} %copy.94, f32[8,2,2,128,32]{3,4,2,1,0:T(8,128)} %copy.93, f32[8,2,2,128,32]{3,4,2,1,0:T(8,128)} %copy.92, f32[8,2,2,128,32]{3,4,2,1,0:T(8,128)} %copy.91, f32[8,2,2,128,32]{3,4,2,1,0:T(8,128)} %copy.90, f32[8,2,2,128,32]{3,4,2,1,0:T(8,128)} %copy.89, ...), kind=kOutput, calls=%fused_computation.35 | convolution fusion | flops 102633472 | bytes 4736000 | tf_op jit(solution)/shard_map/dbisn,jink->bkdjs/dot_general | solution.py:38
  92.3 16.8 %all_to_all.24 = f32[64,8,2,128]{3,1,2,0:T(8,128)S(1)} all-to-all(f32[64,8,2,128]{3,1,2,0:T(8,128)S(1)} %copy.61), channel_id=1, replica_groups=mesh['chan'=64,'quad'=2] {'chan'}, dimensions={0} | all-to-all | bytes 1048576 | tf_op jit(solution)/shard_map/all_to_all | solution.py:62
  110.3 3.8 %fusion.12 = (f32[1,512,512,1]{2,1,3,0:T(8,128)S(1)}, f32[1,512,512,1]{2,1,3,0:T(8,128)S(1)}, f32[1,512,512,1]{2,1,3,0:T(8,128)S(1)}) fusion(s32[1,512,512]{2,1,0:T(8,128)S(1)} %copy-done.12), kind=kLoop, calls=%fused_computation.24 | loop fusion | flops 786432 | bytes 4194304 | tf_op jit(solution)/shard_map/stack | solution.py:46
  115.3 4.4 %fusion.8 = f32[1,2,512,256]{3,2,1,0:T(8,128)} fusion(f32[1,1,512,512,2]{3,2,4,1,0:T(8,128)S(1)} %get-tuple-element.29, f32[1,1,512,512,2]{3,2,4,1,0:T(8,128)S(1)} %get-tuple-element.28, f32[1,512,2,128]{3,1,2,0:T(8,128)S(1)} %bitcast.110, f32[1,512,2,128]{3,1,2,0:T(8,128)S(1)} %bitcast.112), kind=kOutput, calls=%fused_computation.14 | convolution fusion | flops 3222536192 | bytes 6291456 | tf_op jit(solution)/shard_map/cvbri,cris->cvbs/dot_general | solution.py:71
  122.6 10.8 %all-gather.3.cloned.1.call-done = f32[1,1024,2,128]{3,1,2,0:T(8,128)} async-done(((f32[1,512,2,128]{3,1,2,0:T(8,128)}), f32[1,1024,2,128]{3,1,2,0:T(8,128)}) %all-gather.3.cloned.1.call-update) | async-done | bytes 1048592 | tf_op jit(solution)/shard_map/all_gather | solution.py:66
  133.4 2.5 %copy.63 = f32[1,1024,2,128]{1,3,2,0:T(8,128)} copy(f32[1,1024,2,128]{3,1,2,0:T(8,128)} %all-gather.3.cloned.1.call-done) | data formatting | bytes 2097152 | tf_op jit(solution)/shard_map/all_gather | solution.py:66
  136.0 2.5 %copy.64 = f32[1,1,1024,256]{3,2,1,0:T(8,128)} copy(f32[1,1,1024,256]{2,3,1,0:T(8,128)} %bitcast.114) | data formatting | bytes 2097152 | tf_op jit(solution)/shard_map/stack;reshape | solution.py:53
  141.0 3.7 %fusion.3 = f32[2,1024,512]{2,1,0:T(8,128)S(1)} fusion(f32[1,1,1024,256]{3,2,1,0:T(8,128)S(1)} %maximum_bitcast_fusion.10, f32[1,1,1024,256]{3,2,1,0:T(8,128)S(1)} %copy-done.10, f32[64,8,2,128]{3,1,2,0:T(8,128)S(1)} %all_to_all.24), kind=kOutput, calls=%fused_computation.6 | convolution fusion | flops 3221749760 | bytes 6815744 | tf_op jit(solution)/shard_map/crk,cvqk->cvrq/dot_general | solution.py:54
  144.7 5.5 %multiply_bitcast_fusion = f32[1,2,512,1024]{2,3,1,0:T(8,128)} fusion(f32[2,1024,512]{2,1,0:T(8,128)S(1)} %fusion.3, f32[1,1,1024,256]{3,2,1,0:T(8,128)S(1)} %maximum_bitcast_fusion.11, f32[1,1,1024,256]{3,2,1,0:T(8,128)S(1)} %copy-done.11, f32[64,8,2,128]{3,1,2,0:T(8,128)S(1)} %all-to-all-done.1), kind=kOutput, calls=%fused_computation.4 | convolution fusion | flops 3223846912 | bytes 11010048 | tf_op jit(solution)/shard_map/crk,cvqk->cvrq/dot_general | solution.py:54
  150.3 5.4 %copy.78 = f32[1,2,512,1024]{3,2,1,0:T(8,128)} copy(f32[1,2,512,1024]{2,3,1,0:T(8,128)} %multiply_bitcast_fusion) | data formatting | bytes 8388608
  155.6 3.9 %reduce-scatter.2.cloned.1.call-done = f32[1,2,256,256]{3,2,1,0:T(8,128)} async-done(((f32[1,2,512,256]{3,2,1,0:T(8,128)}), f32[1,2,256,256]{3,2,1,0:T(8,128)}) %reduce-scatter.2.cloned.1.call-update) | async-done | bytes 524304 | tf_op jit(solution)/shard_map/reduce_scatter | solution.py:72
  (62 shorter events, 30.4 us)
Async XLA Ops:
  17.6 2.3 %copy-start.4 = (f32[8,2,2,128,32]{4,3,2,1,0:T(8,128)S(1)}, f32[8,2,2,128,32]{4,3,2,1,0:T(8,128)}, u32[]{:S(2)}) copy-start(f32[8,2,2,128,32]{4,3,2,1,0:T(8,128)} %get-tuple-element.11) | copy-start | bytes 1572868
  21.3 6.2 %copy-start.2 = (f32[8,2,2,128,32]{4,3,2,1,0:T(8,128)S(1)}, f32[8,2,2,128,32]{4,3,2,1,0:T(8,128)}, u32[]{:S(2)}) copy-start(f32[8,2,2,128,32]{4,3,2,1,0:T(8,128)} %get-tuple-element.16) | copy-start | bytes 1572868
  28.8 6.1 %copy-start = (f32[8,2,2,128,32]{4,3,2,1,0:T(8,128)S(1)}, f32[8,2,2,128,32]{4,3,2,1,0:T(8,128)}, u32[]{:S(2)}) copy-start(f32[8,2,2,128,32]{4,3,2,1,0:T(8,128)} %get-tuple-element.13) | copy-start | bytes 1572868
  31.9 4.4 %copy-start.13 = (f32[8,32]{1,0:T(8,128)S(1)}, f32[8,32]{1,0:T(8,128)}, u32[]{:S(2)}) copy-start(f32[8,32]{1,0:T(8,128)} %param.4) | copy-start | bytes 3076
  40.4 22.8 %all-to-all-start.1 = ((f32[64,8,2,128]{3,1,2,0:T(8,128)}), f32[64,8,2,128]{3,1,2,0:T(8,128)S(1)}, u32[]{:S(2)}, u32[]{:S(2)}) async-start(f32[64,8,2,128]{3,1,2,0:T(8,128)} %copy.74), calls=%async_computation.1 | async-start | bytes 1048576 | tf_op jit(solution)/shard_map/all_to_all | solution.py:62
  50.7 69.0 %all-gather.5.cloned.1.call-start = ((), (), s32[]{:S(2)}) async-start(), calls=%async_computation.4 | async-start | bytes 1572864 | tf_op jit(solution)/shard_map/all_gather | solution.py:66
  64.0 69.4 %all-gather.3.cloned.1.call-start = ((), (), s32[]{:S(2)}) async-start(), calls=%async_computation.3 | async-start | bytes 1572864 | tf_op jit(solution)/shard_map/all_gather | solution.py:66
  70.2 2.5 %copy-start.5 = (f32[8,2,2,128,32]{4,3,2,1,0:T(8,128)S(1)}, f32[8,2,2,128,32]{4,3,2,1,0:T(8,128)}, u32[]{:S(2)}) copy-start(f32[8,2,2,128,32]{4,3,2,1,0:T(8,128)} %get-tuple-element.24) | copy-start | bytes 1572868
  74.1 6.1 %copy-start.3 = (f32[8,2,2,128,32]{4,3,2,1,0:T(8,128)S(1)}, f32[8,2,2,128,32]{4,3,2,1,0:T(8,128)}, u32[]{:S(2)}) copy-start(f32[8,2,2,128,32]{4,3,2,1,0:T(8,128)} %get-tuple-element.21) | copy-start | bytes 1572868
  81.6 6.1 %copy-start.1 = (f32[8,2,2,128,32]{4,3,2,1,0:T(8,128)S(1)}, f32[8,2,2,128,32]{4,3,2,1,0:T(8,128)}, u32[]{:S(2)}) copy-start(f32[8,2,2,128,32]{4,3,2,1,0:T(8,128)} %get-tuple-element.25) | copy-start | bytes 1572868
  92.0 18.2 %copy-start.12 = (s32[1,512,512]{2,1,0:T(8,128)S(1)}, s32[1,512,512]{2,1,0:T(8,128)}, u32[]{:S(2)}) copy-start(s32[1,512,512]{2,1,0:T(8,128)} %param.5) | copy-start | bytes 3145732
  110.0 49.6 %reduce-scatter.2.cloned.1.call-start = ((), (), s32[]{:S(2)}) async-start(), calls=%async_computation.5 | async-start | bytes 1572864 | tf_op jit(solution)/shard_map/reduce_scatter | solution.py:72
  114.1 1.0 copy-start.6
  114.1 1.2 copy-start.7
  122.6 15.9 %copy-start.8 = (f32[1,1024,2,128]{3,1,2,0:T(8,128)S(1)}, f32[1,1024,2,128]{3,1,2,0:T(8,128)}, u32[]{:S(2)}) copy-start(f32[1,1024,2,128]{3,1,2,0:T(8,128)} %all-gather.5.cloned.1.call-done) | copy-start | bytes 3145732
  138.5 1.2 copy-start.9
  139.7 1.2 copy-start.10
  141.0 3.7 %copy-start.11 = (f32[1,1,1024,256]{3,2,1,0:T(8,128)S(1)}, f32[1,1,1024,256]{3,2,1,0:T(8,128)}, u32[]{:S(2)}) copy-start(f32[1,1,1024,256]{3,2,1,0:T(8,128)} %copy.77) | copy-start | bytes 3145732
Sparse Core Ops, SparseCore 0:
  64.1 23.2 all-gather.4
  110.1 23.2 all-gather.2
  135.8 23.6 reduce-scatter.1
where the time goes:
time: 169 us; the launch traced here: 168 us
  local copies, waits for them, and re-layouts  74 us (44%)
  waiting for transfers between devices  26.1 us (15%)
  matrix products  19.5 us (12%)
  blocking collectives  16.8 us (10%)
  between operations  13.9 us (8%)
  starting transfers between devices  10.9 us (6%)
  other arithmetic  6.6 us (4%)
    unnamed x45, local copies, waits for them, and re-layouts  45.8 us
    all_to_all x1, blocking collectives, per_device(): lax.all_to_all(local_part, 'chan', split_axis=0, concat_axis=1, tiled=True)  16.8 us
    slice x2, local copies, waits for them, and re-layouts, filter_bank(): frames[:, :, :, tap_index:tap_index + length, :]  12 us
    all_to_all x1, waiting for transfers between devices, per_device(): lax.all_to_all(local_part, 'chan', split_axis=0, concat_axis=1, tiled=True)  11.4 us
    all_gather x2, waiting for transfers between devices, per_device(): lax.all_gather(own_rows, 'quad', axis=1, tiled=True)  10.8 us
    all_to_all x1, starting transfers between devices, per_device(): lax.all_to_all(local_part, 'chan', split_axis=0, concat_axis=1, tiled=True)  10.3 us
    dot_general x2, matrix products, make_visit(): jnp.einsum('crk,cvqk->cvrq', left_side, right_side, precision=highest)  9.26 us
    dot_general x2, matrix products, filter_bank(): jnp.einsum('dbisn,jink->bkdjs', filtered, dft_matrix(), precision=highest)  5.8 us
  transfers between devices with their start and end apart: 4, of which 3 were waited for; matrix products, arithmetic and copies ran while one was open for 37% of the time, Pallas kernels for 0%

commit v1 on v0

v1 whole, which is shorter than its diff:
```python
import functools
import math

import jax
import jax.numpy as jnp
import numpy as np
from jax import lax
from jax.experimental import pallas as pl
from jax.experimental.pallas import tpu as pltpu
from jax.sharding import PartitionSpec as P

MESH = pl.DeviceIdType.MESH
F32 = jnp.float32
BF16 = jnp.bfloat16
VMEM = pltpu.VMEM
DMA = pltpu.SemaphoreType.DMA

DISHES = 1024
HALF = 512
FINE = 32
TAPS = 8
LEVELS = 256
SPECTRA = 256
PEERS = 128
BEAMS = 256
NT = (((1,), (1,)), ((), ()))


def sine_terms():
    nodes = 64.0 * np.cos((np.arange(400) + 0.5) * np.pi / 800)
    basis = np.stack([nodes ** (2 * i + 1) / 64.0 ** (2 * i + 1) for i in range(6)], 1)
    fit = np.linalg.lstsq(basis, np.sin(np.pi * nodes / 128), rcond=None)[0]
    return [float(fit[i] / 64.0 ** (2 * i + 1)) for i in range(6)]


SINE = sine_terms()


def split(value):
    high = value.astype(BF16)
    return high, (value - high.astype(F32)).astype(BF16)


def steer(level):
    wrapped = (level + 128) % LEVELS - 128
    unit = (64 - jnp.abs(wrapped)).astype(F32)
    square = unit * unit
    total = jnp.full_like(square, SINE[5])
    for term in SINE[4::-1]:
        total = total * square + term
    return total * unit


def peer(step):
    chan = lax.axis_index("chan")
    quad = lax.axis_index("quad")
    me = chan * 2 + quad
    turn = lax.rem(step * (2 * me + 1), PEERS)
    z = lax.rem(quad * 2 + lax.rem(chan // 2, 2) + lax.rem(turn, 4), 4)
    x = lax.rem(chan // 16 + lax.rem(turn // 4, 4), 4)
    y = lax.rem(lax.rem(chan // 4, 4) + lax.rem(turn // 16, 4), 4)
    core = lax.rem(lax.rem(chan, 2) + turn // 64, 2)
    return x * 16 + y * 4 + lax.rem(z, 2) * 2 + core, z // 2


def transform_table():
    row = lax.broadcasted_iota(jnp.int32, (FINE, 128), 0)
    col = lax.broadcasted_iota(jnp.int32, (FINE, 128), 1) % FINE
    angle = ((row * col) % FINE) * (LEVELS // FINE)
    return steer(angle), steer(angle - 64)


def filter_rows(taps):
    wide = jnp.concatenate([taps] * 4, axis=1)
    tap = lax.broadcasted_iota(jnp.int32, (TAPS, 128), 0)
    group = lax.broadcasted_iota(jnp.int32, (TAPS, 128), 1) // FINE
    rows = []
    for f in range(4):
        rows.append(
            [
                jnp.sum(jnp.where(tap == 4 * a + group - f, wide, 0.0), axis=0, keepdims=True)
                for a in range(3)
            ]
        )
    return rows


def spectra_kernel(volt_hbm, taps_ref, phase_hbm, got_ref, gains_hi, gains_lo,
                   volt, lines, bank, send, phase_own, phase_far,
                   load_sem, send_sem, recv_sem, phase_sems):
    chan = lax.axis_index("chan")
    quad = lax.axis_index("quad")

    load = pltpu.make_async_copy(volt_hbm.at[0], volt, load_sem)
    load.start()
    own = pltpu.make_async_copy(phase_hbm.at[0, pl.ds(quad * BEAMS, BEAMS)], phase_own, phase_sems.at[2])
    own.start()

    barrier = pltpu.get_barrier_semaphore()

    def greet(step, carry):
        pl.semaphore_signal(barrier, inc=1, device_id=peer(step), device_id_type=MESH)
        return carry

    lax.fori_loop(1, PEERS, greet, 0)
    pl.semaphore_wait(barrier, PEERS - 1)

    far = pltpu.make_async_remote_copy(
        src_ref=phase_hbm.at[0, pl.ds((1 - quad) * BEAMS, BEAMS)], dst_ref=phase_far,
        send_sem=phase_sems.at[0], recv_sem=phase_sems.at[1],
        device_id=(chan, 1 - quad), device_id_type=MESH)
    far.start()

    cosine, sine = transform_table()
    taps = filter_rows(taps_ref[...])
    for g in range(2):
        for r in range(2):
            for f in range(2):
                tables = (cosine, sine) if r == 0 else (-sine, cosine)
                at = ((g * 2 + r) * 2 + f) * FINE
                for i in range(2):
                    for a in range(3):
                        high, low = split(tables[i] * taps[2 * g + f][a])
                        col = (i * 3 + a) * 128
                        bank[at:at + FINE, col:col + 128] = high
                        bank[at:at + FINE, 768 + col:768 + col + 128] = high
                        bank[at:at + FINE, 1536 + col:1536 + col + 128] = low

    load.wait()
    for d in range(8):
        for b in range(2):
            for r in range(2):
                lines[d, b, r, 0:64, :] = volt[d, b, r, 0:8192].reshape(64, 128)
                lines[d, b, r, 64:72, :] = jnp.zeros((8, 128), F32)
                lines[d, b, r, 64:65, :] = volt[d, b, r, 8192:8320].reshape(1, 128)
                lines[d, b, r, 65:66, 0:96] = volt[d, b, r, 8320:8416].reshape(1, 96)

    lane = lax.broadcasted_iota(jnp.int32, (FINE, 128), 1)
    for b in range(2):
        for h in range(2):
            high_parts = []
            low_parts = []
            for r in range(2):
                for a in range(3):
                    block = jnp.concatenate([lines[4 * h + d, b, r, a:a + 64, :] for d in range(4)], axis=0)
                    high, low = split(block)
                    high_parts.append(high)
                    low_parts.append(low)
            right = jnp.concatenate(high_parts + low_parts + high_parts, axis=1)
            out = lax.dot_general(bank[...], right, NT, preferred_element_type=F32)
            for g in range(2):
                for r in range(2):
                    at = (g * 2 + r) * 2 * FINE
                    for p in range(2):
                        first = out[at:at + FINE, 128 * p:128 * p + 128]
                        second = out[at + FINE:at + 2 * FINE, 128 * p:128 * p + 128]
                        even = jnp.where(lane < 64, first, pltpu.roll(second, 64, 1))
                        odd = jnp.where(lane < 64, pltpu.roll(first, 64, 1), second)
                        part = 2 * g + r
                        send[part, pl.ds(b * 256 + 4 * h + 2 * p, FINE, stride=8), :] = even
                        send[part, pl.ds(b * 256 + 4 * h + 2 * p + 1, FINE, stride=8), :] = odd

    mine = pl.ds(pl.multiple_of(quad * HALF + chan * 8, 8), 8)
    for g in range(2):
        parts = pl.ds(2 * g, 2)

        def push(step, carry):
            to_chan, to_quad = peer(step)
            pltpu.make_async_remote_copy(
                src_ref=send.at[parts, pl.ds(pl.multiple_of(to_chan * 8, 8), 8)], dst_ref=got_ref.at[parts, mine],
                send_sem=send_sem.at[g], recv_sem=recv_sem.at[g],
                device_id=(to_chan, to_quad), device_id_type=MESH).start()
            return carry

        lax.fori_loop(1, PEERS, push, 0)
    for part in range(4):
        got_ref[part, mine, :] = send[part, pl.ds(pl.multiple_of(chan * 8, 8), 8), :]

    def gains(source, half):
        for start in range(0, BEAMS, 32):
            level = source[start:start + 32, :]
            for i in range(2):
                high, low = split(steer(level - 64 * i))
                cols = pl.ds(pl.multiple_of(i * DISHES + half * HALF, HALF), HALF)
                gains_hi[start:start + 32, cols] = high
                gains_lo[start:start + 32, cols] = low

    own.wait()
    gains(phase_own, quad)
    far.wait_recv()
    gains(phase_far, 1 - quad)

    for g in range(2):
        whole = got_ref.at[pl.ds(2 * g, 2), pl.ds(0, (PEERS - 1) * 8)]
        pltpu.make_async_copy(whole, whole, recv_sem.at[g]).wait()
        pltpu.make_async_copy(whole, whole, send_sem.at[g]).wait()
    far.wait_send()


def turned(block):
    parts = []
    for g in range(2):
        parts += [block[:, g * 256 + 128:g * 256 + 256], -block[:, g * 256:g * 256 + 128]]
    return jnp.concatenate(parts, axis=1)


def joined(ref, rows):
    return jnp.concatenate([ref[part, rows, :] for part in range(4)], axis=1)


def product_kernel(got_ref, gains_hi, gains_lo, vis_ref, power_ref, left, right):
    quad = lax.axis_index("quad")

    @pl.when(pl.program_id(0) == 0)
    def _():
        for start in range(0, DISHES, 128):
            rows = slice(start, start + 128)
            high, low = split(joined(got_ref, rows))
            right[rows, 0:512] = high
            right[rows, 512:1024] = low
            right[rows, 1024:1536] = high
        for start in range(0, HALF, 128):
            rows = pl.ds(pl.multiple_of(quad * HALF + start, 128), 128)
            block = joined(got_ref, rows) * (1.0 / SPECTRA)
            high, low = split(block)
            left[start:start + 128, 0:512] = high
            left[start:start + 128, 512:1024] = high
            left[start:start + 128, 1024:1536] = low
            high, low = turned(high), turned(low)
            left[HALF + start:HALF + start + 128, 0:512] = high
            left[HALF + start:HALF + start + 128, 512:1024] = high
            left[HALF + start:HALF + start + 128, 1024:1536] = low

    cols = pl.ds(pl.multiple_of(pl.program_id(0) * 256, 256), 256)
    out = lax.dot_general(left[...], right[cols, :], NT, preferred_element_type=F32)
    vis_ref[0, 0] = out[0:HALF]
    vis_ref[0, 1] = out[HALF:]

    @pl.when(pl.program_id(0) == 0)
    def _():
        high = right[:, 0:512]
        low = right[:, 512:1024]
        both_high = jnp.concatenate([high, turned(high)], axis=0)
        both_low = jnp.concatenate([low, turned(low)], axis=0)
        beams = jnp.dot(gains_hi[...], both_high, preferred_element_type=F32)
        beams += jnp.dot(gains_hi[...], both_low, preferred_element_type=F32)
        beams += jnp.dot(gains_lo[...], both_high, preferred_element_type=F32)
        beams = beams * beams
        power = jnp.concatenate(
            [beams[:, 0:128] + beams[:, 128:256], beams[:, 256:384] + beams[:, 384:512]], axis=1
        ) * (1.0 / DISHES)
        source = lax.broadcasted_iota(jnp.int32, (SPECTRA, SPECTRA), 0)
        target = lax.broadcasted_iota(jnp.int32, (SPECTRA, SPECTRA), 1)
        order = (4 * (source % 64) + source // 64 == target).astype(BF16)
        high = power.astype(BF16)
        rest = power - high.astype(F32)
        middle, low = split(rest)
        power_ref[0] = (
            jnp.dot(high, order, preferred_element_type=F32)
            + jnp.dot(middle, order, preferred_element_type=F32)
            + jnp.dot(low, order, preferred_element_type=F32)
        )


def per_device(voltages, filter_taps, phases):
    any_space = pl.BlockSpec(memory_space=pl.ANY)
    vmem_space = pl.BlockSpec(memory_space=VMEM)
    got, gains_hi, gains_lo = pl.pallas_call(
        spectra_kernel,
        name="spectra",
        out_shape=(
            jax.ShapeDtypeStruct((4, DISHES, 128), F32),
            jax.ShapeDtypeStruct((BEAMS, 2 * DISHES), BF16),
            jax.ShapeDtypeStruct((BEAMS, 2 * DISHES), BF16),
        ),
        in_specs=[any_space, vmem_space, any_space],
        out_specs=(vmem_space, vmem_space, vmem_space),
        scratch_shapes=[
            VMEM((8, 2, 2, 8416), F32),
            VMEM((8, 2, 2, 72, 128), F32),
            VMEM((256, 2304), BF16),
            VMEM((4, 512, 128), F32),
            VMEM((BEAMS, HALF), jnp.int32),
            VMEM((BEAMS, HALF), jnp.int32),
            DMA,
            DMA((2,)),
            DMA((2,)),
            DMA((3,)),
        ],
        compiler_params=pltpu.CompilerParams(
            collective_id=0, has_side_effects=True, vmem_limit_bytes=24 * 2**20
        ),
    )(voltages, filter_taps, phases)
    return pl.pallas_call(
        product_kernel,
        name="products",
        grid=(4,),
        out_shape=(
            jax.ShapeDtypeStruct((1, 2, HALF, DISHES), F32),
            jax.ShapeDtypeStruct((1, BEAMS, SPECTRA), F32),
        ),
        in_specs=[vmem_space, vmem_space, vmem_space],
        out_specs=(
            pl.BlockSpec((1, 2, HALF, 256), lambda i: (0, 0, 0, i)),
            pl.BlockSpec((1, BEAMS, SPECTRA), lambda i: (0, 0, 0)),
        ),
        scratch_shapes=[VMEM((DISHES, 1536), BF16), VMEM((DISHES, 1536), BF16)],
        compiler_params=pltpu.CompilerParams(vmem_limit_bytes=32 * 2**20),
    )(got, gains_hi, gains_lo)


def solution(mesh):
    return jax.shard_map(
        per_device,
        mesh=mesh,
        in_specs=(P("quad", "chan", None, None, None), P(), P("chan", None, "quad")),
        out_specs=(P("chan", None, "quad", None), P("chan", "quad", None)),
        check_vma=False,
    )
```

time: 169 us -> 65.1 us (0.39)
  local copies, waits for them, and re-layouts: 74 us -> 3.14 us
  Pallas kernels: 0 us -> 61.1 us
  waiting for transfers between devices: 26.1 us -> 0 us
  matrix products: 19.5 us -> 0 us
  blocking collectives: 16.8 us -> 0 us
  between operations: 13.9 us -> 0.65 us
  starting transfers between devices: 10.9 us -> 0 us
  other arithmetic: 6.6 us -> 0 us
    pallas_call x0 -> x2, Pallas kernels: none -> 61.1 us  [the longest x1 53 us: per_device(): pl.pallas_call(spectra_kernel, name='spectra', out_shape=(jax.ShapeDtypeS...]
    unnamed x45 -> x6, local copies, waits for them, and re-layouts: 45.8 us -> 3.14 us
    dot_general x5 -> x0, matrix products: 19.5 us -> none  [the longest x2 9.26 us: make_visit(): jnp.einsum('crk,cvqk->cvrq', left_side, right_side, precision=highest)]
    all_to_all x1 -> x0, blocking collectives: 16.8 us -> none  [per_device(): lax.all_to_all(local_part, 'chan', split_axis=0, concat_axis=1, tiled=True)]
    slice x3 -> x0, local copies, waits for them, and re-layouts: 14.1 us -> none  [the longest x2 12 us: filter_bank(): frames[:, :, :, tap_index:tap_index + length, :]]
    all_to_all x1 -> x0, waiting for transfers between devices: 11.4 us -> none  [per_device(): lax.all_to_all(local_part, 'chan', split_axis=0, concat_axis=1, tiled=True)]
    all_gather x2 -> x0, waiting for transfers between devices: 10.8 us -> none  [per_device(): lax.all_gather(own_rows, 'quad', axis=1, tiled=True)]
    all_to_all x1 -> x0, starting transfers between devices: 10.3 us -> none  [per_device(): lax.all_to_all(local_part, 'chan', split_axis=0, concat_axis=1, tiled=True)]
  transfers between devices with their start and end apart: 4 -> 0, of which waited for: 3 -> 0; matrix products, arithmetic and copies ran while one was open for 37% -> 0% of each run, Pallas kernels for 0% -> 0%
where the time goes in v1:
time: 65.1 us; the launch traced here: 64.9 us
  Pallas kernels  61.1 us (94%)
  local copies, waits for them, and re-layouts  3.14 us (5%)
    pallas_call x1, Pallas kernels, per_device(): pl.pallas_call(spectra_kernel, name='spectra', out_shape=(jax.ShapeDtypeS...  53 us
    pallas_call x1, Pallas kernels, per_device(): pl.pallas_call(product_kernel, name='products', grid=(4,), out_shape=(jax...  8.06 us
    unnamed x6, local copies, waits for them, and re-layouts  3.14 us

profile of v1, /device:TPU:1, one launch (start us, length us, event | category | flops | bytes accessed | tf_op | source)
XLA Modules:
  0.0 64.9 jit_solution(7045249981257427486)
XLA Ops:
  0.6 0.0 copy-start
  0.6 1.2 %copy-done = f32[1,8,2,2,8416]{4,3,2,1,0:T(2,128)S(1)} copy-done((f32[1,8,2,2,8416]{4,3,2,1,0:T(2,128)S(1)}, f32[1,8,2,2,8416]{4,3,2,1,0:T(2,128)}, u32[]{:S(2)}) %copy-start) | copy-done | bytes 1077272
  1.9 0.0 copy-start.1
  1.9 1.2 %copy-done.1 = s32[1,512,512]{2,1,0:T(8,128)S(1)} copy-done((s32[1,512,512]{2,1,0:T(8,128)S(1)}, s32[1,512,512]{2,1,0:T(8,128)}, u32[]{:S(2)}) %copy-start.1) | copy-done | bytes 1048600
  3.1 0.0 copy-start.2
  3.1 0.7 %copy-done.2 = f32[8,32]{1,0:T(8,128)S(1)} copy-done((f32[8,32]{1,0:T(8,128)S(1)}, f32[8,32]{1,0:T(8,128)}, u32[]{:S(2)}) %copy-start.2) | copy-done | bytes 1048
  3.8 53.0 %spectra.1 = (f32[4,1024,128]{2,1,0:T(8,128)S(1)}, bf16[256,2048]{1,0:T(8,128)(2,1)S(1)}, bf16[256,2048]{1,0:T(8,128)(2,1)S(1)}) custom-call(f32[1,8,2,2,8416]{4,3,2,1,0:T(2,128)S(1)} %copy-done, f32[8,32]{1,0:T(8,128)S(1)} %copy-done.2, s32[1,512,512]{2,1,0:T(8,128)S(1)} %copy-done.1), custom_call_target="tpu_custom_call" | custom-call | tf_op jit(solution)/shard_map/spectra/pallas_call | solution.py:268
  56.8 8.1 %products.1 = (f32[1,2,512,1024]{3,2,1,0:T(8,128)}, f32[1,256,256]{2,1,0:T(8,128)}) custom-call(f32[4,1024,128]{2,1,0:T(8,128)S(1)} %get-tuple-element.5.got_ref, bf16[256,2048]{1,0:T(8,128)(2,1)S(1)} %get-tuple-element.6.gains_hi, bf16[256,2048]{1,0:T(8,128)(2,1)S(1)} %get-tuple-element.7.gains_lo), custom_call_target="tpu_custom_call" | custom-call | tf_op jit(solution)/shard_map/products/pallas_call | solution.py:294
Async XLA Ops:
  0.6 1.2 %copy-start = (f32[1,8,2,2,8416]{4,3,2,1,0:T(2,128)S(1)}, f32[1,8,2,2,8416]{4,3,2,1,0:T(2,128)}, u32[]{:S(2)}) copy-start(f32[1,8,2,2,8416]{4,3,2,1,0:T(2,128)} %volt_hbm.1) | copy-start | bytes 3231748
  1.9 1.2 %copy-start.1 = (s32[1,512,512]{2,1,0:T(8,128)S(1)}, s32[1,512,512]{2,1,0:T(8,128)}, u32[]{:S(2)}) copy-start(s32[1,512,512]{2,1,0:T(8,128)} %phase_hbm.1) | copy-start | bytes 3145732
  3.1 0.7 %copy-start.2 = (f32[8,32]{1,0:T(8,128)S(1)}, f32[8,32]{1,0:T(8,128)}, u32[]{:S(2)}) copy-start(f32[8,32]{1,0:T(8,128)} %taps_ref.1) | copy-start | bytes 3076

commit v2 on v1

v2 whole, which is shorter than its diff:
```python
import functools
import math

import jax
import jax.numpy as jnp
import numpy as np
from jax import lax
from jax.experimental import pallas as pl
from jax.experimental.pallas import tpu as pltpu
from jax.sharding import PartitionSpec as P

MESH = pl.DeviceIdType.MESH
F32 = jnp.float32
BF16 = jnp.bfloat16
VMEM = pltpu.VMEM
DMA = pltpu.SemaphoreType.DMA

DISHES = 1024
HALF = 512
FINE = 32
TAPS = 8
LEVELS = 256
SPECTRA = 256
PEERS = 128
BEAMS = 256
NT = (((1,), (1,)), ((), ()))


def sine_terms():
    nodes = 64.0 * np.cos((np.arange(400) + 0.5) * np.pi / 800)
    basis = np.stack([nodes ** (2 * i + 1) / 64.0 ** (2 * i + 1) for i in range(6)], 1)
    fit = np.linalg.lstsq(basis, np.sin(np.pi * nodes / 128), rcond=None)[0]
    return [float(fit[i] / 64.0 ** (2 * i + 1)) for i in range(6)]


SINE = sine_terms()


def split(value):
    high = value.astype(BF16)
    return high, (value - high.astype(F32)).astype(BF16)


def steer(level):
    wrapped = (level + 128) % LEVELS - 128
    unit = (64 - jnp.abs(wrapped)).astype(F32)
    square = unit * unit
    total = jnp.full_like(square, SINE[5])
    for term in SINE[4::-1]:
        total = total * square + term
    return total * unit


def each_peer(visit, after):
    chan = lax.axis_index("chan")
    quad = lax.axis_index("quad")
    x, y, z, core = chan // 16, (chan // 4) % 4, quad * 2 + (chan // 2) % 2, chan % 2
    ends = []
    for dc in range(2):
        for dz in (2, 1, 3, 0):
            there = (z + dz) % 4
            ends.append((dz + dc, (there % 2) * 2 + (core + dc) % 2, there // 2))

    def step(t, here):
        column = ((x + t % 4) % 4) * 16 + ((y + t // 4) % 4) * 4
        for shift, low, there in ends:
            if shift or not here:
                visit(t, column + low, there)

    step(0, True)
    after(0)

    def body(t, carry):
        step(t, False)
        after(t)
        return carry

    lax.fori_loop(1, 16, body, 0)


def transform_table():
    row = lax.broadcasted_iota(jnp.int32, (FINE, 128), 0)
    col = lax.broadcasted_iota(jnp.int32, (FINE, 128), 1) % FINE
    angle = ((row * col) % FINE) * (LEVELS // FINE)
    return steer(angle), steer(angle - 64)


def filter_rows(taps):
    wide = jnp.concatenate([taps] * 4, axis=1)
    tap = lax.broadcasted_iota(jnp.int32, (TAPS, 128), 0)
    group = lax.broadcasted_iota(jnp.int32, (TAPS, 128), 1) // FINE
    rows = []
    for f in range(4):
        rows.append(
            [
                jnp.sum(jnp.where(tap == 4 * a + group - f, wide, 0.0), axis=0, keepdims=True)
                for a in range(3)
            ]
        )
    return rows


def spectra_kernel(volt_hbm, taps_hbm, phase_hbm, sums_ref, left, right, own_hi, own_lo, far_hi, far_lo, power_ref,
                   volt, taps_ref, lines, bank, send, got, phase_own, phase_far,
                   load_sem, taps_sem, send_sem, recv_sem, own_sem, far_send, far_recv):
    chan = lax.axis_index("chan")
    quad = lax.axis_index("quad")

    load = pltpu.make_async_copy(volt_hbm.at[0], volt, load_sem)
    load.start()
    load_taps = pltpu.make_async_copy(taps_hbm, taps_ref, taps_sem)
    load_taps.start()
    own = pltpu.make_async_copy(phase_hbm.at[0, pl.ds(quad * BEAMS, BEAMS)], phase_own, own_sem)
    own.start()

    barrier = pltpu.get_barrier_semaphore()

    def greet(step, to_chan, to_quad):
        pl.semaphore_signal(barrier, inc=1, device_id=(to_chan, to_quad), device_id_type=MESH)

    each_peer(greet, lambda step: None)

    cosine, sine = transform_table()
    load_taps.wait()
    taps = filter_rows(taps_ref[...])
    for g in range(2):
        for r in range(2):
            for f in range(2):
                tables = (cosine, sine) if r == 0 else (-sine, cosine)
                at = ((g * 2 + r) * 2 + f) * FINE
                for i in range(2):
                    for a in range(3):
                        high, low = split(tables[i] * taps[2 * g + f][a])
                        col = (i * 3 + a) * 128
                        bank[at:at + FINE, col:col + 128] = high
                        bank[at:at + FINE, 768 + col:768 + col + 128] = high
                        bank[at:at + FINE, 1536 + col:1536 + col + 128] = low

    load.wait()
    for d in range(8):
        for b in range(2):
            for r in range(2):
                lines[d, b, r, 0:64, :] = volt[d, b, r, 0:8192].reshape(64, 128)
                lines[d, b, r, 64:72, :] = jnp.zeros((8, 128), F32)
                lines[d, b, r, 64:65, :] = volt[d, b, r, 8192:8320].reshape(1, 128)
                lines[d, b, r, 65:66, 0:96] = volt[d, b, r, 8320:8416].reshape(1, 96)

    lane = lax.broadcasted_iota(jnp.int32, (FINE, 128), 1)
    for b in range(2):
        for h in range(2):
            high_parts = []
            low_parts = []
            for r in range(2):
                for a in range(3):
                    block = jnp.concatenate([lines[4 * h + d, b, r, a:a + 64, :] for d in range(4)], axis=0)
                    high, low = split(block)
                    high_parts.append(high)
                    low_parts.append(low)
            window = jnp.concatenate(high_parts + low_parts + high_parts, axis=1)
            out = lax.dot_general(bank[...], window, NT, preferred_element_type=F32)
            for g in range(2):
                for r in range(2):
                    part = 2 * g + r
                    for p in range(2):
                        cols = slice(128 * p, 128 * p + 128)
                        first = out[part * 64:part * 64 + FINE, cols]
                        second = out[part * 64 + FINE:part * 64 + 2 * FINE, cols]
                        even = jnp.where(lane < 64, first, pltpu.roll(second, 64, 1))
                        odd = jnp.where(lane < 64, pltpu.roll(first, 64, 1), second)
                        at = b * 1024 + part * 8 + 4 * h + 2 * p
                        send[pl.ds(at, FINE, stride=32), :] = even
                        send[pl.ds(at + 1, FINE, stride=32), :] = odd

    slot = quad * 64 + chan

    def far(piece):
        return pltpu.make_async_remote_copy(
            src_ref=phase_hbm.at[0, pl.ds(pl.multiple_of((1 - quad) * BEAMS + piece * 8, 8), 8)],
            dst_ref=phase_far.at[pl.ds(pl.multiple_of(piece * 8, 8), 8)],
            send_sem=far_send, recv_sem=far_recv,
            device_id=(chan, 1 - quad), device_id_type=MESH)

    def far_all(sem):
        pltpu.make_async_copy(phase_far, phase_far, sem).wait()

    pl.semaphore_wait(barrier, PEERS - 1)
    for g in range(2):

        def push(step, to_chan, to_quad):
            pltpu.make_async_remote_copy(
                src_ref=send.at[pl.ds(pl.multiple_of(to_chan * 32 + 16 * g, 16), 16)],
                dst_ref=got.at[slot, pl.ds(16 * g, 16)],
                send_sem=send_sem.at[g], recv_sem=recv_sem.at[g],
                device_id=(to_chan, to_quad), device_id_type=MESH).start()

        each_peer(push, lambda step: far(16 * g + step).start())
    got[slot] = send[pl.ds(pl.multiple_of(chan * 32, 32), 32), :]

    own.wait()
    gains(phase_own, own_hi, own_lo)
    arrived(got, recv_sem.at[0], 0)
    prepare(got, 0, quad, left, right)

    def product(tile, carry):
        cols = pl.ds(pl.multiple_of(tile * 256, 256), 256)
        sums_ref[:, cols] = lax.dot_general(left[...], right[cols, :], NT, preferred_element_type=F32)
        return carry

    lax.fori_loop(0, 4, product, 0)
    far_all(far_recv)
    gains(phase_far, far_hi, far_lo)
    power_ref[...] = powered(quad, own_hi, own_lo, far_hi, far_lo, right)

    arrived(got, recv_sem.at[1], 1)
    prepare(got, 1, quad, left, right)
    for g in range(2):
        arrived(got, send_sem.at[g], g)
    far_all(far_send)


def gains(source, high_ref, low_ref):
    for start in range(0, source.shape[0], 32):
        level = source[start:start + 32, :]
        for i in range(2):
            high, low = split(steer(level - 64 * i))
            high_ref[start:start + 32, i * HALF:i * HALF + HALF] = high
            low_ref[start:start + 32, i * HALF:i * HALF + HALF] = low


def arrived(got, sem, g):
    whole = got.at[pl.ds(0, PEERS - 1), pl.ds(16 * g, 16)]
    pltpu.make_async_copy(whole, whole, sem).wait()


def turned(block):
    return jnp.concatenate([block[:, 128:256], -block[:, 0:128]], axis=1)


def prepare(got, g, quad, left, right):
    for start in range(0, DISHES, 128):
        rows = slice(start, start + 128)
        block = got[start // 8:start // 8 + 16, 16 * g:16 * g + 16, :]
        high, low = split(
            jnp.concatenate([block[:, 0:8].reshape(128, 128), block[:, 8:16].reshape(128, 128)], axis=1))
        right[rows, 0:256] = high
        right[rows, 256:512] = low
        right[rows, 512:768] = high
    for start in range(0, HALF, 128):
        rows = pl.ds(pl.multiple_of(quad * HALF + start, 128), 128)
        high = right[rows, 0:256] * (1.0 / SPECTRA)
        low = right[rows, 256:512] * (1.0 / SPECTRA)
        left[start:start + 128, 0:256] = high
        left[start:start + 128, 256:512] = high
        left[start:start + 128, 512:768] = low
        high, low = turned(high), turned(low)
        left[HALF + start:HALF + start + 128, 0:256] = high
        left[HALF + start:HALF + start + 128, 256:512] = high
        left[HALF + start:HALF + start + 128, 512:768] = low


def steered(gains_hi, gains_lo, right, rows):
    high = right[rows, 0:256]
    low = right[rows, 256:512]
    both_high = jnp.concatenate([high, turned(high)], axis=0)
    both_low = jnp.concatenate([low, turned(low)], axis=0)
    beams = jnp.dot(gains_hi[...], both_high, preferred_element_type=F32)
    beams += jnp.dot(gains_hi[...], both_low, preferred_element_type=F32)
    beams += jnp.dot(gains_lo[...], both_high, preferred_element_type=F32)
    return beams


def powered(quad, own_hi, own_lo, far_hi, far_lo, right):
    near = pl.ds(pl.multiple_of(quad * HALF, HALF), HALF)
    other = pl.ds(pl.multiple_of((1 - quad) * HALF, HALF), HALF)
    beams = steered(own_hi, own_lo, right, near) + steered(far_hi, far_lo, right, other)
    beams = beams * beams
    return (beams[:, 0:128] + beams[:, 128:256]) * (1.0 / DISHES)


def finish_kernel(sums_ref, left, right, own_hi, own_lo, far_hi, far_lo, first_power, vis_hbm, power_hbm,
                  vis_ref, power_ref, vis_sem, power_sem):
    quad = lax.axis_index("quad")
    copies = []
    for tile in range(4):
        cols = pl.ds(tile * 256, 256)
        vis_ref[tile] = sums_ref[:, cols] + lax.dot_general(left[...], right[cols, :], NT, preferred_element_type=F32)
        for i in range(2):
            copies.append(pltpu.make_async_copy(
                vis_ref.at[tile, pl.ds(i * HALF, HALF)], vis_hbm.at[0, i, :, cols], vis_sem.at[2 * tile + i]))
            copies[-1].start()

    power = jnp.concatenate([first_power[...], powered(quad, own_hi, own_lo, far_hi, far_lo, right)], axis=1)
    source = lax.broadcasted_iota(jnp.int32, (SPECTRA, SPECTRA), 0)
    target = lax.broadcasted_iota(jnp.int32, (SPECTRA, SPECTRA), 1)
    order = (4 * (source % 64) + source // 64 == target).astype(BF16)
    high = power.astype(BF16)
    middle, low = split(power - high.astype(F32))
    power_ref[...] = (
        jnp.dot(high, order, preferred_element_type=F32)
        + jnp.dot(middle, order, preferred_element_type=F32)
        + jnp.dot(low, order, preferred_element_type=F32)
    )
    copy = pltpu.make_async_copy(power_ref, power_hbm.at[0], power_sem)
    copy.start()
    copy.wait()
    for copy in copies:
        copy.wait()


def per_device(voltages, filter_taps, phases):
    hbm_space = pl.BlockSpec(memory_space=pltpu.HBM)
    vmem_space = pl.BlockSpec(memory_space=VMEM)
    made = pl.pallas_call(
        spectra_kernel,
        name="spectra",
        out_shape=(
            jax.ShapeDtypeStruct((DISHES, DISHES), F32),
            jax.ShapeDtypeStruct((DISHES, 768), BF16),
            jax.ShapeDtypeStruct((DISHES, 768), BF16),
            jax.ShapeDtypeStruct((BEAMS, DISHES), BF16),
            jax.ShapeDtypeStruct((BEAMS, DISHES), BF16),
            jax.ShapeDtypeStruct((BEAMS, DISHES), BF16),
            jax.ShapeDtypeStruct((BEAMS, DISHES), BF16),
            jax.ShapeDtypeStruct((BEAMS, 128), F32),
        ),
        in_specs=[hbm_space] * 3,
        out_specs=(vmem_space,) * 8,
        scratch_shapes=[
            VMEM((8, 2, 2, 8416), F32),
            VMEM((TAPS, FINE), F32),
            VMEM((8, 2, 2, 72, 128), F32),
            VMEM((256, 2304), BF16),
            VMEM((2048, 128), F32),
            VMEM((PEERS, 32, 128), F32),
            VMEM((BEAMS, HALF), jnp.int32),
            VMEM((BEAMS, HALF), jnp.int32),
            DMA,
            DMA,
            DMA((2,)),
            DMA((2,)),
            DMA,
            DMA,
            DMA,
        ],
        compiler_params=pltpu.CompilerParams(
            collective_id=0, has_side_effects=True, vmem_limit_bytes=28 * 2**20
        ),
    )(*[pltpu.with_memory_space_constraint(x, pltpu.HBM) for x in (voltages, filter_taps, phases)])
    return pl.pallas_call(
        finish_kernel,
        name="finish",
        out_shape=(
            jax.ShapeDtypeStruct((1, 2, HALF, DISHES), F32),
            jax.ShapeDtypeStruct((1, BEAMS, SPECTRA), F32),
        ),
        in_specs=[vmem_space] * 8,
        out_specs=(hbm_space, hbm_space),
        scratch_shapes=[VMEM((4, DISHES, 256), F32), VMEM((BEAMS, SPECTRA), F32), DMA((8,)), DMA],
        compiler_params=pltpu.CompilerParams(vmem_limit_bytes=16 * 2**20),
    )(*made)


def solution(mesh):
    return jax.shard_map(
        per_device,
        mesh=mesh,
        in_specs=(P("quad", "chan", None, None, None), P(), P("chan", None, "quad")),
        out_specs=(P("chan", None, "quad", None), P("chan", "quad", None)),
        check_vma=False,
    )
```

time: 65.1 us -> 54.2 us (0.83)
  Pallas kernels: 61.1 us -> 53.4 us
  local copies, waits for them, and re-layouts: 3.14 us -> 0 us
    pallas_call x1, Pallas kernels: 8.06 us -> 3.95 us  [per_device(): pl.pallas_call(finish_kernel, name='finish', out_shape=(jax.ShapeDtypeStr...]
    pallas_call x1, Pallas kernels: 53 us -> 49.5 us  [per_device(): pl.pallas_call(spectra_kernel, name='spectra', out_shape=(jax.ShapeDtypeS...]
    unnamed x6 -> x0, local copies, waits for them, and re-layouts: 3.14 us -> none
where the time goes in v2:
time: 54.2 us; the launch traced here: 54.1 us
  Pallas kernels  53.4 us (99%)
  between operations  0.64 us (1%)
    pallas_call x1, Pallas kernels, per_device(): pl.pallas_call(spectra_kernel, name='spectra', out_shape=(jax.ShapeDtypeS...  49.5 us
    pallas_call x1, Pallas kernels, per_device(): pl.pallas_call(finish_kernel, name='finish', out_shape=(jax.ShapeDtypeStr...  3.95 us

profile of v2, /device:TPU:1, one launch (start us, length us, event | category | flops | bytes accessed | tf_op | source)
XLA Modules:
  0.0 54.1 jit_solution(1101943459980955633)
XLA Ops:
  0.6 49.5 %spectra.1 = (f32[1024,1024]{1,0:T(8,128)S(1)}, bf16[1024,768]{1,0:T(8,128)(2,1)S(1)}, bf16[1024,768]{1,0:T(8,128)(2,1)S(1)}, bf16[256,1024]{1,0:T(8,128)(2,1)S(...) custom-call(f32[1,8,2,2,8416]{4,3,2,1,0:T(2,128)} %volt_hbm.1, ...), custom_call_target="tpu_custom_call" | custom-call | tf_op jit(solution)/shard_map/spectra/pallas_call | solution.py:313
  50.1 4.0 %finish.1 = (f32[1,2,512,1024]{3,2,1,0:T(8,128)}, f32[1,256,256]{2,1,0:T(8,128)}) custom-call(f32[1024,1024]{1,0:T(8,128)S(1)} %get-tuple-element.10.sums_ref, bf16[1024,768]{1,0:T(8,128)(2,1)S(1)} %get-tuple-element.11.left, bf16[1024,768]{1,0:T(8,128)(2,1)S(1)} %get-tuple-element.12.right, bf16[256,1024]{1,0:T(8,128)(2,1)S(1)} %get-tuple-element.13.own_hi, ...), custom_call_target="tpu_custom_call" | custom-call | tf_op jit(solution)/shard_map/finish/pallas_call | solution.py:349

commit v3 on v2

--- a/solution.py
+++ b/solution.py
@@ -23,6 +23,8 @@
 SPECTRA = 256
 PEERS = 128
 BEAMS = 256
+LOTS = (0, 128, 256)
+CHUNKS = ((0, 3), (3, 4))
 NT = (((1,), (1,)), ((), ()))
 
 
@@ -100,8 +102,8 @@
     return rows
 
 
-def spectra_kernel(volt_hbm, taps_hbm, phase_hbm, sums_ref, left, right, own_hi, own_lo, far_hi, far_lo, power_ref,
-                   volt, taps_ref, lines, bank, send, got, phase_own, phase_far,
+def spectra_kernel(volt_hbm, taps_hbm, phase_hbm, sums_ref, left, both_all, own_hi, own_lo, far_hi, far_lo, power_ref,
+                   volt, taps_ref, lines, bank, send, got, first_all, first_left, second_left, phase_own, phase_far,
                    load_sem, taps_sem, send_sem, recv_sem, own_sem, far_send, far_recv):
     chan = lax.axis_index("chan")
     quad = lax.axis_index("quad")
@@ -123,18 +125,17 @@
     cosine, sine = transform_table()
     load_taps.wait()
     taps = filter_rows(taps_ref[...])
-    for g in range(2):
+    for f in range(4):
         for r in range(2):
-            for f in range(2):
-                tables = (cosine, sine) if r == 0 else (-sine, cosine)
-                at = ((g * 2 + r) * 2 + f) * FINE
-                for i in range(2):
-                    for a in range(3):
-                        high, low = split(tables[i] * taps[2 * g + f][a])
-                        col = (i * 3 + a) * 128
-                        bank[at:at + FINE, col:col + 128] = high
-                        bank[at:at + FINE, 768 + col:768 + col + 128] = high
-                        bank[at:at + FINE, 1536 + col:1536 + col + 128] = low
+            tables = (cosine, sine) if r == 0 else (-sine, cosine)
+            at = (f * 2 + r) * FINE
+            for i in range(2):
+                for a in range(3):
+                    high, low = split(tables[i] * taps[f][a])
+                    col = (i * 3 + a) * 128
+                    bank[at:at + FINE, col:col + 128] = high
+                    bank[at:at + FINE, 768 + col:768 + col + 128] = high
+                    bank[at:at + FINE, 1536 + col:1536 + col + 128] = low
 
     load.wait()
     for d in range(8):
@@ -158,64 +159,81 @@
                     low_parts.append(low)
             window = jnp.concatenate(high_parts + low_parts + high_parts, axis=1)
             out = lax.dot_general(bank[...], window, NT, preferred_element_type=F32)
-            for g in range(2):
-                for r in range(2):
-                    part = 2 * g + r
-                    for p in range(2):
-                        cols = slice(128 * p, 128 * p + 128)
-                        first = out[part * 64:part * 64 + FINE, cols]
-                        second = out[part * 64 + FINE:part * 64 + 2 * FINE, cols]
-                        even = jnp.where(lane < 64, first, pltpu.roll(second, 64, 1))
-                        odd = jnp.where(lane < 64, pltpu.roll(first, 64, 1), second)
-                        at = b * 1024 + part * 8 + 4 * h + 2 * p
-                        send[pl.ds(at, FINE, stride=32), :] = even
-                        send[pl.ds(at + 1, FINE, stride=32), :] = odd
+            for f in range(4):
+                for p in range(2):
+                    cols = slice(128 * p, 128 * p + 128)
+                    first = out[f * 64:f * 64 + FINE, cols]
+                    second = out[f * 64 + FINE:f * 64 + 2 * FINE, cols]
+                    even = jnp.where(lane < 64, first, pltpu.roll(second, 64, 1))
+                    odd = jnp.where(lane < 64, pltpu.roll(first, 64, 1), second)
+                    at = b * 1024 + f * 8 + 4 * h + 2 * p
+                    send[pl.ds(at, FINE, stride=32), :] = even
+                    send[pl.ds(at + 1, FINE, stride=32), :] = odd
 
     slot = quad * 64 + chan
 
-    def far(piece):
+    def far(piece, lot):
         return pltpu.make_async_remote_copy(
             src_ref=phase_hbm.at[0, pl.ds(pl.multiple_of((1 - quad) * BEAMS + piece * 8, 8), 8)],
             dst_ref=phase_far.at[pl.ds(pl.multiple_of(piece * 8, 8), 8)],
-            send_sem=far_send, recv_sem=far_recv,
+            send_sem=far_send, recv_sem=far_recv.at[lot],
             device_id=(chan, 1 - quad), device_id_type=MESH)
 
-    def far_all(sem):
-        pltpu.make_async_copy(phase_far, phase_far, sem).wait()
+    def far_lot(lot):
+        rows = phase_far.at[pl.ds(LOTS[lot], LOTS[lot + 1] - LOTS[lot])]
+        pltpu.make_async_copy(rows, rows, far_recv.at[lot]).wait()
+        rows = pl.ds(LOTS[lot], LOTS[lot + 1] - LOTS[lot])
+        gains(phase_far.at[rows], far_hi.at[rows], far_lo.at[rows])
 
     pl.semaphore_wait(barrier, PEERS - 1)
-    for g in range(2):
+    for g, (start, stop) in enumerate(CHUNKS):
+        count = 8 * (stop - start)
 
         def push(step, to_chan, to_quad):
             pltpu.make_async_remote_copy(
-                src_ref=send.at[pl.ds(pl.multiple_of(to_chan * 32 + 16 * g, 16), 16)],
-                dst_ref=got.at[slot, pl.ds(16 * g, 16)],
+                src_ref=send.at[pl.ds(pl.multiple_of(to_chan * 32 + 8 * start, 8), count)],
+                dst_ref=got.at[slot, pl.ds(8 * start, count)],
                 send_sem=send_sem.at[g], recv_sem=recv_sem.at[g],
                 device_id=(to_chan, to_quad), device_id_type=MESH).start()
 
-        each_peer(push, lambda step: far(16 * g + step).start())
+        def between(step):
+            if g == 0:
+                lot = jnp.where(16 * step < LOTS[1], 0, 1)
+                far(2 * step, lot).start()
+                far(2 * step + 1, lot).start()
+
+        each_peer(push, between)
     got[slot] = send[pl.ds(pl.multiple_of(chan * 32, 32), 32), :]
 
     own.wait()
     gains(phase_own, own_hi, own_lo)
     arrived(got, recv_sem.at[0], 0)
-    prepare(got, 0, quad, left, right)
-
-    def product(tile, carry):
+    prepare(got, (0, 1), quad, first_all, first_left)
+    prepare(got, (2,), quad, both_all, second_left)
+
+    def product_first(tile, carry):
         cols = pl.ds(pl.multiple_of(tile * 256, 256), 256)
-        sums_ref[:, cols] = lax.dot_general(left[...], right[cols, :], NT, preferred_element_type=F32)
+        sums_ref[:, cols] = product([(first_left, first_all, 0, 2), (second_left, both_all, 0, 1)], cols)
         return carry
 
-    lax.fori_loop(0, 4, product, 0)
-    far_all(far_recv)
-    gains(phase_far, far_hi, far_lo)
-    power_ref[...] = powered(quad, own_hi, own_lo, far_hi, far_lo, right)
-
+    lax.fori_loop(0, 4, product_first, 0)
+    near = pl.ds(pl.multiple_of(quad * HALF, HALF), HALF)
+    other = pl.ds(pl.multiple_of((1 - quad) * HALF, HALF), HALF)
+    part = steered(own_hi, own_lo, first_all, near)
+
+    def far_beams(lot):
+        far_lot(lot)
+        rows = slice(LOTS[lot], LOTS[lot + 1])
+        powers = squared(part[rows] + steered(far_hi.at[rows], far_lo.at[rows], first_all, other))
+        power_ref[rows] = side_by_side(powers[:, 0:128], powers[:, 128:256])
+
+    far_beams(0)
+    far_beams(1)
     arrived(got, recv_sem.at[1], 1)
-    prepare(got, 1, quad, left, right)
+    prepare(got, (3,), quad, both_all, left)
     for g in range(2):
         arrived(got, send_sem.at[g], g)
-    far_all(far_send)
+    pltpu.make_async_copy(phase_far, phase_far, far_send).wait()
 
 
 def gains(source, high_ref, low_ref):
@@ -228,68 +246,86 @@
 
 
 def arrived(got, sem, g):
-    whole = got.at[pl.ds(0, PEERS - 1), pl.ds(16 * g, 16)]
+    start, stop = CHUNKS[g]
+    whole = got.at[pl.ds(0, PEERS - 1), pl.ds(8 * start, 8 * (stop - start))]
     pltpu.make_async_copy(whole, whole, sem).wait()
 
 
-def turned(block):
-    return jnp.concatenate([block[:, 128:256], -block[:, 0:128]], axis=1)
-
-
-def prepare(got, g, quad, left, right):
-    for start in range(0, DISHES, 128):
-        rows = slice(start, start + 128)
-        block = got[start // 8:start // 8 + 16, 16 * g:16 * g + 16, :]
-        high, low = split(
-            jnp.concatenate([block[:, 0:8].reshape(128, 128), block[:, 8:16].reshape(128, 128)], axis=1))
-        right[rows, 0:256] = high
-        right[rows, 256:512] = low
-        right[rows, 512:768] = high
-    for start in range(0, HALF, 128):
-        rows = pl.ds(pl.multiple_of(quad * HALF + start, 128), 128)
-        high = right[rows, 0:256] * (1.0 / SPECTRA)
-        low = right[rows, 256:512] * (1.0 / SPECTRA)
-        left[start:start + 128, 0:256] = high
-        left[start:start + 128, 256:512] = high
-        left[start:start + 128, 512:768] = low
-        high, low = turned(high), turned(low)
-        left[HALF + start:HALF + start + 128, 0:256] = high
-        left[HALF + start:HALF + start + 128, 256:512] = high
-        left[HALF + start:HALF + start + 128, 512:768] = low
-
-
-def steered(gains_hi, gains_lo, right, rows):
-    high = right[rows, 0:256]
-    low = right[rows, 256:512]
-    both_high = jnp.concatenate([high, turned(high)], axis=0)
-    both_low = jnp.concatenate([low, turned(low)], axis=0)
+def prepare(got, parts, quad, everything, left):
+    width = 128 * len(parts)
+    lane = lax.broadcasted_iota(jnp.int32, (128, 128), 1)
+    for i, f in enumerate(parts):
+        col = 128 * (f % 2)
+        for start in range(0, DISHES, 128):
+            rows = slice(start, start + 128)
+            block = got[start // 8:start // 8 + 16, 8 * f:8 * f + 8, :].reshape(128, 128)
+            moved = pltpu.roll(block, 64, 1)
+            high, low = split(block)
+            everything[rows, col:col + 128] = high
+            everything[rows, 256 + col:256 + col + 128] = low
+            high, low = split(jnp.where(lane < 64, moved, -moved))
+            everything[rows, 512 + col:512 + col + 128] = high
+            everything[rows, 768 + col:768 + col + 128] = low
+        for start in range(0, HALF, 128):
+            rows = pl.ds(pl.multiple_of(quad * HALF + start, 128), 128)
+            for turn in range(2):
+                at = turn * HALF + start
+                source = 512 * turn + col
+                left[at:at + 128, 128 * i:128 * i + 128] = everything[rows, source:source + 128] * (1.0 / SPECTRA)
+                left[at:at + 128, width + 128 * i:width + 128 * i + 128] = (
+                    everything[rows, 256 + source:256 + source + 128] * (1.0 / SPECTRA))
+
+
+def product(terms, cols):
+    lhs = []
+    rhs = []
+    for left, everything, first, parts in terms:
+        width = 128 * parts
+        at = 128 * first
+        high = left[:, 0:width]
+        far_high = everything[cols, at:at + width]
+        lhs += [high, high, left[:, width:2 * width]]
+        rhs += [far_high, everything[cols, 256 + at:256 + at + width], far_high]
+    return lax.dot_general(
+        jnp.concatenate(lhs, axis=1), jnp.concatenate(rhs, axis=1), NT, preferred_element_type=F32)
+
+
+def steered(gains_hi, gains_lo, everything, rows):
+    both_high = jnp.concatenate([everything[rows, 0:256], everything[rows, 512:768]], axis=0)
+    both_low = jnp.concatenate([everything[rows, 256:512], everything[rows, 768:1024]], axis=0)
     beams = jnp.dot(gains_hi[...], both_high, preferred_element_type=F32)
     beams += jnp.dot(gains_hi[...], both_low, preferred_element_type=F32)
     beams += jnp.dot(gains_lo[...], both_high, preferred_element_type=F32)
     return beams
 
 
-def powered(quad, own_hi, own_lo, far_hi, far_lo, right):
-    near = pl.ds(pl.multiple_of(quad * HALF, HALF), HALF)
-    other = pl.ds(pl.multiple_of((1 - quad) * HALF, HALF), HALF)
-    beams = steered(own_hi, own_lo, right, near) + steered(far_hi, far_lo, right, other)
-    beams = beams * beams
-    return (beams[:, 0:128] + beams[:, 128:256]) * (1.0 / DISHES)
-
-
-def finish_kernel(sums_ref, left, right, own_hi, own_lo, far_hi, far_lo, first_power, vis_hbm, power_hbm,
+def squared(beams):
+    beams = beams * beams * (1.0 / DISHES)
+    return jnp.concatenate(
+        [beams[:, i:i + 128] + pltpu.roll(beams[:, i:i + 128], 64, 1) for i in (0, 128)], axis=1)
+
+
+def side_by_side(first, second):
+    lane = lax.broadcasted_iota(jnp.int32, first.shape, 1)
+    return jnp.where(lane < 64, first, second)
+
+
+def finish_kernel(sums_ref, left, everything, own_hi, own_lo, far_hi, far_lo, first_power, vis_hbm, power_hbm,
                   vis_ref, power_ref, vis_sem, power_sem):
     quad = lax.axis_index("quad")
     copies = []
     for tile in range(4):
         cols = pl.ds(tile * 256, 256)
-        vis_ref[tile] = sums_ref[:, cols] + lax.dot_general(left[...], right[cols, :], NT, preferred_element_type=F32)
+        vis_ref[tile] = sums_ref[:, cols] + product([(left, everything, 1, 1)], cols)
         for i in range(2):
             copies.append(pltpu.make_async_copy(
                 vis_ref.at[tile, pl.ds(i * HALF, HALF)], vis_hbm.at[0, i, :, cols], vis_sem.at[2 * tile + i]))
             copies[-1].start()
 
-    power = jnp.concatenate([first_power[...], powered(quad, own_hi, own_lo, far_hi, far_lo, right)], axis=1)
+    near = pl.ds(pl.multiple_of(quad * HALF, HALF), HALF)
+    other = pl.ds(pl.multiple_of((1 - quad) * HALF, HALF), HALF)
+    powers = squared(steered(own_hi, own_lo, everything, near) + steered(far_hi, far_lo, everything, other))
+    power = jnp.concatenate([first_power[...], side_by_side(powers[:, 0:128], powers[:, 128:256])], axis=1)
     source = lax.broadcasted_iota(jnp.int32, (SPECTRA, SPECTRA), 0)
     target = lax.broadcasted_iota(jnp.int32, (SPECTRA, SPECTRA), 1)
     order = (4 * (source % 64) + source // 64 == target).astype(BF16)
@@ -315,8 +351,8 @@
         name="spectra",
         out_shape=(
             jax.ShapeDtypeStruct((DISHES, DISHES), F32),
-            jax.ShapeDtypeStruct((DISHES, 768), BF16),
-            jax.ShapeDtypeStruct((DISHES, 768), BF16),
+            jax.ShapeDtypeStruct((DISHES, 256), BF16),
+            jax.ShapeDtypeStruct((DISHES, 1024), BF16),
             jax.ShapeDtypeStruct((BEAMS, DISHES), BF16),
             jax.ShapeDtypeStruct((BEAMS, DISHES), BF16),
             jax.ShapeDtypeStruct((BEAMS, DISHES), BF16),
@@ -332,6 +368,9 @@
             VMEM((256, 2304), BF16),
             VMEM((2048, 128), F32),
             VMEM((PEERS, 32, 128), F32),
+            VMEM((DISHES, 1024), BF16),
+            VMEM((DISHES, 512), BF16),
+            VMEM((DISHES, 256), BF16),
             VMEM((BEAMS, HALF), jnp.int32),
             VMEM((BEAMS, HALF), jnp.int32),
             DMA,
@@ -340,7 +379,7 @@
             DMA((2,)),
             DMA,
             DMA,
-            DMA,
+            DMA((2,)),
         ],
         compiler_params=pltpu.CompilerParams(
             collective_id=0, has_side_effects=True, vmem_limit_bytes=28 * 2**20

time: 54.2 us -> 52.7 us (0.972)
  Pallas kernels: 53.4 us -> 52 us
    pallas_call x1, Pallas kernels: 49.5 us -> 48.6 us  [per_device(): pl.pallas_call(spectra_kernel, name='spectra', out_shape=(jax.ShapeDtypeS...]
    pallas_call x1, Pallas kernels: 3.95 us -> 3.31 us  [per_device(): pl.pallas_call(finish_kernel, name='finish', out_shape=(jax.ShapeDtypeStr...]
where the time goes in v3:
time: 52.7 us; the launch traced here: 52.6 us
  Pallas kernels  52 us (99%)
  between operations  0.64 us (1%)
    pallas_call x1, Pallas kernels, per_device(): pl.pallas_call(spectra_kernel, name='spectra', out_shape=(jax.ShapeDtypeS...  48.6 us
    pallas_call x1, Pallas kernels, per_device(): pl.pallas_call(finish_kernel, name='finish', out_shape=(jax.ShapeDtypeStr...  3.31 us

profile of v3, /device:TPU:1, one launch (start us, length us, event | category | flops | bytes accessed | tf_op | source)
XLA Modules:
  0.0 52.6 jit_solution(15902501237759690742)
XLA Ops:
  0.6 48.6 %spectra.1 = (f32[1024,1024]{1,0:T(8,128)S(1)}, bf16[1024,256]{1,0:T(8,128)(2,1)S(1)}, bf16[1024,1024]{1,0:T(8,128)(2,1)S(1)}, bf16[256,1024]{1,0:T(8,128)(2,1)S...) custom-call(f32[1,8,2,2,8416]{4,3,2,1,0:T(2,128)} %volt_hbm.1, ...), custom_call_target="tpu_custom_call" | custom-call | tf_op jit(solution)/shard_map/spectra/pallas_call | solution.py:349
  49.3 3.3 %finish.1 = (f32[1,2,512,1024]{3,2,1,0:T(8,128)}, f32[1,256,256]{2,1,0:T(8,128)}) custom-call(f32[1024,1024]{1,0:T(8,128)S(1)} %get-tuple-element.10.sums_ref, bf16[1024,256]{1,0:T(8,128)(2,1)S(1)} %get-tuple-element.11.left, bf16[1024,1024]{1,0:T(8,128)(2,1)S(1)} %get-tuple-element.12.everything, bf16[256,1024]{1,0:T(8,128)(2,1)S(1)} %get-tuple-element.13.own_hi, ...), custom_call_target="tpu_custom_call" | custom-call | tf_op jit(solution)/shard_map/finish/pallas_call | solution.py:388
